TPU v7x, 32 devices: a whole 2x2x4 slice. The times are simulated.
32 devices in a mesh: stretch: 8 (over z, y), section: 4 (over x, core).
Axes of the slice: x: 2, y: 2, z: 4, core: 2. Of those that a mesh axis runs over, the one named last changes fastest.
Arguments:
- hidden: bfloat16 [4, 4096, 4096], P('section', 'stretch'), may hold values from -64 to 64
- norm_gain: float32 [4, 4096], P('section'), may hold values from 0.5 to 1.5
- queries: bfloat16 [4, 4096, 2048], P('section', 'stretch'), may hold values from -110 to 110
- cache: bfloat16 [4, 128, 32, 4096], P('section', 'stretch'), may hold values from -35 to 35
- nbr_shard: int32 [64, 2], P('stretch'), may hold values from 0 to 7, as said below
- nbr_slot: int32 [64, 2], P('stretch'), may hold values from 0 to 15
- grad_heads: bfloat16 [4, 4096, 2048], P('section', 'stretch'), may hold values from -24 to 24
- grad_out: bfloat16 [4, 4096, 4096], P('section', 'stretch'), may hold values from -3 to 3
- query_weight: bfloat16 [4, 4096, 2048], P('section', 'stretch'), may hold values from -0.09375 to 0.09375
Outputs:
- section_grads: bfloat16 [4, 4096, 4096], P('section', 'stretch')
Inputs may be any that keep to these rules, and one draw needn't show every extreme that they name: `nbr_shard`: the 2 shards of a stretch differ. In the 8 stretches of one device (aligned blocks of rows) no shard is named more than 2 times; one shard is named exactly 2 times in every such block.
All inputs are finite; a program needn't handle non-finite values.
Results may differ from a plain program's by a relative error of at most 0.0067.
Values may be sent and summed in bfloat16 or wider, within the bound.
A program may use at most 192 MiB of HBM per device.

v0:
```python
import jax
import jax.numpy as jnp
from jax import lax
from jax.sharding import PartitionSpec as P

HEAD_DIM = 128
STRETCH = 64


norm_eps = 1e-05


def passed_along(value, axis, steps):
    count = lax.axis_size(axis)
    pairs = [(source, (source + steps) % count) for source in range(count)]
    return lax.ppermute(value, axis, pairs)


def slot_ranks(owners):
    count = owners.shape[0]
    positions = jnp.arange(count)
    same_owner = owners[:, None] == owners[None, :]
    earlier = positions[:, None] > positions[None, :]
    return jnp.sum((same_owner & earlier).astype(jnp.int32), axis=1)


def request_table(owners, slot_rank, slot_ids, shards, capacity):
    matched = (owners[:, None, None] == jnp.arange(shards)[None, :, None]) & (
        slot_rank[:, None, None] == jnp.arange(capacity)[None, None, :]
    )
    return jnp.sum(jnp.where(matched, slot_ids[:, None, None] + 1, 0), axis=0) - 1


def local(
    hidden, norm_gain, queries, cache, nbr_shard, nbr_slot, grad_heads, grad_out, query_weight
):
    shards = lax.axis_size("stretch")
    tokens_here = hidden.shape[1]
    qwidth = queries.shape[2]
    head_count = qwidth // HEAD_DIM
    stretches_here = nbr_shard.shape[0]
    neighbours = nbr_shard.shape[1]
    capacity = (neighbours * stretches_here + shards - 1) // shards
    nbr_span = cache.shape[2]
    cache_table = cache[0]
    owners = nbr_shard.reshape(-1)
    slot_ids = nbr_slot.reshape(-1)
    slot_rank = slot_ranks(owners)
    wanted = request_table(owners, slot_rank, slot_ids, shards, capacity)
    picked = cache_table[
        jnp.maximum(lax.all_to_all(wanted, "stretch", split_axis=0, concat_axis=0, tiled=True), 0)
    ]
    fetched = lax.all_to_all(picked, "stretch", split_axis=0, concat_axis=0, tiled=True)
    gathered_rows = fetched[owners, slot_rank].reshape(
        stretches_here, neighbours * nbr_span, 2 * qwidth
    )
    factor = HEAD_DIM ** (-0.5)
    key_heads = gathered_rows[:, :, :qwidth].reshape(
        stretches_here, neighbours * nbr_span, head_count, HEAD_DIM
    )
    value_heads = gathered_rows[:, :, qwidth:].reshape(
        stretches_here, neighbours * nbr_span, head_count, HEAD_DIM
    )
    query_heads = queries[0].reshape(stretches_here, STRETCH, head_count, HEAD_DIM)
    grad_split = grad_heads[0].reshape(stretches_here, STRETCH, head_count, HEAD_DIM)
    scores = (
        jnp.einsum("cqhd,ckhd->chqk", query_heads, key_heads, preferred_element_type=jnp.float32)
        * factor
    )
    row_max = jnp.max(scores, axis=-1, keepdims=True)
    exp_scores = jnp.exp(scores - row_max)
    attn_probs = exp_scores / jnp.sum(exp_scores, axis=-1, keepdims=True)
    dprob = jnp.einsum(
        "cqhd,ckhd->chqk", grad_split, value_heads, preferred_element_type=jnp.float32
    )
    row_inner = jnp.sum(attn_probs * dprob, axis=-1, keepdims=True)
    dscore = (factor * attn_probs * (dprob - row_inner)).astype(jnp.bfloat16)
    query_grad = jnp.einsum(
        "chqk,ckhd->cqhd", dscore, key_heads, preferred_element_type=jnp.float32
    )
    query_grad = query_grad.astype(jnp.bfloat16).reshape(tokens_here, qwidth)
    weight_rows = query_weight[0]
    norm_grad = lax.dot_general(
        query_grad,
        lax.all_gather(weight_rows, "stretch", axis=0, tiled=True),
        (((1,), (1,)), ((), ())),
        preferred_element_type=jnp.float32,
    )
    values_in = hidden[0].astype(jnp.float32)
    inv_rms = lax.rsqrt(jnp.mean(values_in * values_in, axis=-1, keepdims=True) + norm_eps)
    normed = values_in * inv_rms
    scaled_grad = norm_grad * norm_gain[0][None, :]
    mean_term = jnp.mean(scaled_grad * normed, axis=-1, keepdims=True)
    layer_result = grad_out[0].astype(jnp.float32) + inv_rms * (scaled_grad - normed * mean_term)
    outgoing = layer_result.astype(jnp.bfloat16)[None]
    return passed_along(outgoing, "section", -1)


def solution(mesh):
    in_specs = (
        P("section", "stretch", None),
        P("section", None),
        P("section", "stretch", None),
        P("section", "stretch", None, None),
        P("stretch", None),
        P("stretch", None),
        P("section", "stretch", None),
        P("section", "stretch", None),
        P("section", "stretch", None),
    )
    out_specs = P("section", "stretch", None)
    return jax.shard_map(local, mesh=mesh, in_specs=in_specs, out_specs=out_specs, check_vma=False)
```

profile of v0, /device:TPU:1, one launch (start us, length us, event | category | flops | bytes accessed | tf_op | source)
XLA Modules:
  0.0 398.9 jit_solution(5161499486092333889)
XLA Ops:
  6.5 0.7 all-gather.3.cloned.1.call-update
  7.3 0.8 copy.42
  8.1 0.7 broadcast_add_fusion
  8.9 0.2 convert_reduce_fusion
  9.4 11.5 %all_to_all.11 = s32[8,1,2]{2,1,0:T(1,128)S(1)} all-to-all(s32[8,1,2]{2,1,0:T(1,128)S(1)} %copy.44), channel_id=1, replica_groups=mesh['stretch'=8,'section'=4] {'stretch'}, dimensions={0} | all-to-all | bytes 128 | tf_op jit(solution)/shard_map/all_to_all | solution.py:51
  21.0 5.4 %gather_fusion = bf16[16,32,4096]{2,1,0:T(8,128)(2,1)} fusion(bf16[16,32,4096]{2,1,0:T(8,128)(2,1)} %bitcast.87, s32[1024]{0:T(1024)S(1)} %pad_clamp_fusion), kind=kCustom, calls=%fused_computation | custom fusion | bytes 8388672 | tf_op jit(solution)/shard_map/gather | solution.py:50
  26.4 4.7 %all-to-all-start.1 = ((bf16[8,2,32,4096]{3,2,1,0:T(8,128)(2,1)}), bf16[8,2,32,4096]{3,2,1,0:T(8,128)(2,1)}, u32[]{:S(2)}, u32[]{:S(2)}) async-start(bf16[8,2,32,4096]{3,2,1,0:T(8,128)(2,1)} %bitcast.84), calls=%async_computation.1 | async-start | bytes 8388608 | tf_op jit(solution)/shard_map/all_to_all | solution.py:53
  31.2 2.0 copy.58
  33.2 2.0 copy.57
  35.2 0.9 fusion.11
  36.1 170.9 %all-to-all-done.1 = bf16[8,2,32,4096]{3,2,1,0:T(8,128)(2,1)} async-done(((bf16[8,2,32,4096]{3,2,1,0:T(8,128)(2,1)}), bf16[8,2,32,4096]{3,2,1,0:T(8,128)(2,1)}, u32[]{:S(2)}, u32[]{:S(2)}) %all-to-all-start.1) | async-done | bytes 4194336 | tf_op jit(solution)/shard_map/all_to_all | solution.py:53
  207.0 5.0 %gather_fusion.1 = bf16[16,32,4096]{2,1,0:T(8,128)(2,1)} fusion(bf16[8,2,32,4096]{3,2,1,0:T(8,128)(2,1)} %all-to-all-done.1, s32[16]{0:T(128)S(1)} %fusion.49), kind=kCustom, calls=%fused_computation.1 | custom fusion | bytes 8388736 | tf_op jit(solution)/shard_map/gather | solution.py:54
  212.0 2.8 slice_bitcast_fusion.1
  214.8 3.2 fusion.26
  218.1 3.2 fusion.29
  221.2 8.4 %fusion.13 = (f32[8,16,64]{2,1,0:T(8,128)S(1)}, f32[8,16,64,64]{2,3,1,0:T(8,128)}) fusion(f32[8,16,64,64]{3,2,1,0:T(8,128)} %fusion.26, f32[8,16,64,64]{3,2,1,0:T(8,128)} %fusion.29), kind=kOutput, calls=%fused_computation.19 | output fusion | flops 3154046 | bytes 6324224 | tf_op jit(solution)/shard_map/div | solution.py:72
  229.7 4.6 %convert_bitcast_fusion = bf16[8,64,16,128]{3,1,2,0:T(8,128)(2,1)S(1)} fusion(f32[8,16,64,64]{3,2,1,0:T(8,128)} %fusion.26, f32[8,16,64,64]{2,3,1,0:T(8,128)} %get-tuple-element.8, f32[8,16,64]{2,1,0:T(8,128)S(1)} %get-tuple-element.7, bf16[8,8,16,8,128]{4,3,2,1,0:T(8,128)(2,1)S(1)} %get-tuple-element.5), kind=kOutput, calls=%fused_computation.42 | convolution fusion | flops 137363456 | bytes 8421376 | tf_op jit(solution)/shard_map/chqk,ckhd->cqhd/dot_general | solution.py:78
  234.3 2.8 copy.53
  237.0 82.3 %all-gather.3.cloned.1.call-done = bf16[1,4096,2048]{2,1,0:T(8,128)(2,1)} async-done(((bf16[1,512,2048]{2,1,0:T(8,128)(2,1)}), bf16[1,4096,2048]{2,1,0:T(8,128)(2,1)}) %all-gather.3.cloned.1.call-update) | async-done | bytes 16777232 | tf_op jit(solution)/shard_map/all_gather | solution.py:85
  319.4 16.3 %fusion.6 = (f32[512]{0:T(512)S(1)}, f32[512,4096]{1,0:T(8,128)}) fusion(bf16[1,512,4096]{2,1,0:T(8,128)(2,1)} %param.9, f32[4096]{0:T(1024)S(1)} %bitcast.91, f32[512]{0:T(512)S(1)} %add_rsqrt_fusion, bf16[1,4096,2048]{2,1,0:T(8,128)(2,1)} %all-gather.3.cloned.1.call-done, bf16[64,8,16,128]{3,2,1,0:T(8,128)(2,1)} %bitcast.90), kind=kOutput, calls=%fused_computation.10 | convolution fusion | flops 8600420352 | bytes 31477760 | tf_op jit(solution)/shard_map/dot_general | solution.py:83
  335.7 6.3 %fusion.12 = bf16[1,512,4096]{2,1,0:T(8,128)(2,1)S(1)} fusion(f32[512,4096]{1,0:T(8,128)} %get-tuple-element.10, bf16[1,512,4096]{2,1,0:T(8,128)(2,1)} %param.16, bf16[1,512,4096]{2,1,0:T(8,128)(2,1)S(1)} %copy-done.1, f32[512]{0:T(512)S(1)} %broadcast_multiply_fusion, f32[4096]{0:T(1024)S(1)} %bitcast.92, f32[512]{0:T(512)S(1)} %add_rsqrt_fusion), kind=kLoop, calls=%fused_computation.16 | loop fusion | flops 18874368 | bytes 20992000 | tf_op jit(solution)/shard_map/broadcast_in_dim | solution.py:95
  342.0 0.5 collective-permute-start
  342.5 47.5 %collective-permute-done = bf16[1,512,4096]{2,1,0:T(8,128)(2,1)S(1)} collective-permute-done((bf16[1,512,4096]{2,1,0:T(8,128)(2,1)S(1)}, bf16[1,512,4096]{2,1,0:T(8,128)(2,1)S(1)}, u32[]{:S(2)}, u32[]{:S(2)}) %collective-permute-start) | collective-permute-done | bytes 4194336 | tf_op jit(solution)/shard_map/ppermute | solution.py:16
  390.0 2.0 copy.83
  (30 shorter events, 0.8 us)
Async XLA Ops:
  6.5 312.8 %all-gather.3.cloned.1.call-start = ((), (), s32[]{:S(2)}) async-start(), calls=%async_computation.2 | async-start | bytes 18874368 | tf_op jit(solution)/shard_map/all_gather | solution.py:85
  26.4 4.8 %copy-start.4 = (bf16[1,512,2048]{2,1,0:T(8,128)(2,1)S(1)}, bf16[1,512,2048]{2,1,0:T(8,128)(2,1)}, u32[]{:S(2)}) copy-start(bf16[1,512,2048]{2,1,0:T(8,128)(2,1)} %param.15) | copy-start | bytes 6291460
  26.4 180.5 %all-to-all-start.1 = ((bf16[8,2,32,4096]{3,2,1,0:T(8,128)(2,1)}), bf16[8,2,32,4096]{3,2,1,0:T(8,128)(2,1)}, u32[]{:S(2)}, u32[]{:S(2)}) async-start(bf16[8,2,32,4096]{3,2,1,0:T(8,128)(2,1)} %bitcast.84), calls=%async_computation.1 | async-start | bytes 8388608 | tf_op jit(solution)/shard_map/all_to_all | solution.py:53
  31.2 2.0 copy-start.5
  31.2 4.0 copy-start
  212.0 2.9 copy-start.3
  214.8 3.2 copy-start.2
  234.3 85.1 %copy-start.6 = (f32[1,4096]{1,0:T(1,128)S(1)}, f32[1,4096]{1,0:T(1,128)}, u32[]{:S(2)}) copy-start(f32[1,4096]{1,0:T(1,128)} %param.10) | copy-start | bytes 49156
  319.4 16.3 %copy-start.1 = (bf16[1,512,4096]{2,1,0:T(8,128)(2,1)S(1)}, bf16[1,512,4096]{2,1,0:T(8,128)(2,1)}, u32[]{:S(2)}) copy-start(bf16[1,512,4096]{2,1,0:T(8,128)(2,1)} %param.9) | copy-start | bytes 12582916
  342.0 48.0 %collective-permute-start = (bf16[1,512,4096]{2,1,0:T(8,128)(2,1)S(1)}, bf16[1,512,4096]{2,1,0:T(8,128)(2,1)S(1)}, u32[]{:S(2)}, u32[]{:S(2)}) collective-permute-start(bf16[1,512,4096]{2,1,0:T(8,128)(2,1)S(1)} %fusion.12), channel_id=1, source_target_pairs={{0,3},{1,0},{2,1},{3,2},{4,7},{5,4},{6,5},{7,6},{8,11},{9,8},{10,9... | collective-permute-start | bytes 12582920 | tf_op jit(solution)/shard_map/ppermute | solution.py:16
Sparse Core Ops, SparseCore 0:
  9.5 309.8 all-gather.2
where the time goes:
time: 399 us
  waiting for transfers between devices  301 us (75%)
  matrix products  27.3 us (7%)
  local copies, waits for them, and re-layouts  23.3 us (6%)
  other arithmetic  16.7 us (4%)
  between operations  13.5 us (3%)
  blocking collectives  11.5 us (3%)
  starting transfers between devices  5.19 us (1%)
    all_to_all x1, waiting for transfers between devices, local(): lax.all_to_all(picked, 'stretch', split_axis=0, concat_axis=0, tiled=True)  171 us
    all_gather x1, waiting for transfers between devices, local(): lax.all_gather(weight_rows, 'stretch', axis=0, tiled=True)  82.3 us
    ppermute x1, waiting for transfers between devices, passed_along(): return lax.ppermute(value, axis, pairs)  47.5 us
    dot_general x1, matrix products, local(): lax.dot_general(query_grad, lax.all_gather(weight_rows, 'stretch', axis=0...  16.3 us
    all_to_all x1, blocking collectives, local(): lax.all_to_all(wanted, 'stretch', split_axis=0, concat_axis=0, tiled=True)  11.5 us
    unnamed x19, local copies, waits for them, and re-layouts  9.57 us
    div x1, other arithmetic, local(): attn_probs = exp_scores / jnp.sum(exp_scores, axis=-1, keepdims=True)  8.44 us
  transfers between devices with their start and end apart: 3, of which 3 were waited for; matrix products, arithmetic and copies ran while one was open for 11% of the time, Pallas kernels for 0%

commit v1 on v0

v1 whole, which is shorter than its diff:
```python
import functools

import jax
import jax.numpy as jnp
from jax import lax
from jax.experimental import pallas as pl
from jax.experimental.pallas import tpu as pltpu
from jax.sharding import PartitionSpec as P

HEAD_DIM = 128
STRETCH = 64
MESH = pl.DeviceIdType.MESH
NT = (((1,), (1,)), ((), ()))
NN = (((1,), (0,)), ((), ()))

norm_eps = 1e-05


def slot_ranks(owners):
    count = owners.shape[0]
    positions = jnp.arange(count)
    same_owner = owners[:, None] == owners[None, :]
    earlier = positions[:, None] > positions[None, :]
    return jnp.sum((same_owner & earlier).astype(jnp.int32), axis=1)


def request_table(owners, slot_rank, slot_ids, shards, capacity):
    matched = (owners[:, None, None] == jnp.arange(shards)[None, :, None]) & (
        slot_rank[:, None, None] == jnp.arange(capacity)[None, None, :]
    )
    return jnp.sum(jnp.where(matched, slot_ids[:, None, None], 0), axis=0)


def kernel(
    shards, sections, capacity, parts,
    wanted, place, gain, hidden, queries, cache, grads, grad_out, weight,
    out,
    req, req_s, cache_v, picked, fetched, q_v, gh_v, wbuf, qg, stage, g_in, hid_in, gout_in,
    load_sem, req_send, req_recv, kv_send, kv_recv, w_send, w_recv, qg_send, qg_recv,
    g_send, g_recv, x_send, x_recv, out_sem,
):
    me = lax.axis_index("stretch")
    sec = lax.axis_index("section")
    before = lax.rem(sec + sections - 1, sections)
    after = lax.rem(sec + 1, sections)
    side = lax.rem(me, 2)
    spot = me // 2
    partner = me + 1 - 2 * side
    line = shards // 2
    tokens, qwidth = queries.shape
    width = hidden.shape[1]
    heads = qwidth // HEAD_DIM
    stretches = tokens // STRETCH
    span = cache.shape[1]
    piece = weight.shape[0] // parts

    def remote(src, dst, ssem, rsem, stretch, section):
        return pltpu.make_async_remote_copy(
            src_ref=src, dst_ref=dst, send_sem=ssem, recv_sem=rsem,
            device_id=(stretch, section), device_id_type=MESH,
        )

    cache_load = pltpu.make_async_copy(cache, cache_v, load_sem.at[0])
    q_load = pltpu.make_async_copy(queries, q_v, load_sem.at[1])
    gh_load = pltpu.make_async_copy(grads, gh_v, load_sem.at[2])
    cache_load.start()

    barrier = pltpu.get_barrier_semaphore()

    @pl.loop(1, shards)
    def _(off):
        pl.semaphore_signal(
            barrier, inc=1, device_id=(lax.rem(me + off, shards), sec), device_id_type=MESH
        )

    for section in (before, after):
        for stretch in (me, partner):
            pl.semaphore_signal(barrier, inc=1, device_id=(stretch, section), device_id_type=MESH)
    pl.semaphore_wait(barrier, shards + 3)

    def req_copy(to, slot):
        return remote(wanted.at[to], req.at[slot], req_send.at[to], req_recv.at[slot], to, sec)

    @pl.loop(1, shards)
    def _(off):
        req_copy(lax.rem(me + off, shards), me).start()

    q_load.start()
    gh_load.start()
    own_loads = [
        pltpu.make_async_copy(
            weight.at[pl.ds(c * piece, piece)], wbuf.at[spot * parts + c], load_sem.at[4 + c]
        )
        for c in range(parts)
    ]
    for load in own_loads:
        load.start()
    req[me] = wanted[me]
    cache_load.wait()

    @pl.loop(1, shards)
    def _(off):
        req_copy(lax.rem(me + off, shards), lax.rem(me + off, shards)).wait_recv()

    req_load = pltpu.make_async_copy(req, req_s, load_sem.at[3])
    req_load.start()
    req_load.wait()

    def kv_copy(to, slot):
        return remote(
            picked.at[pl.ds(to * capacity, capacity)],
            fetched.at[pl.ds(slot * capacity, capacity)],
            kv_send.at[to], kv_recv.at[slot], to, sec,
        )

    @pl.loop(1, shards)
    def _(off):
        to = lax.rem(me + off, shards)
        for k in range(capacity):
            picked[to * capacity + k] = cache_v[req_s[to, 0, k]]
        kv_copy(to, me).start()

    for k in range(capacity):
        fetched[me * capacity + k] = cache_v[req_s[me, 0, k]]

    def w_copy(way, block, c):
        unit = block * parts + c
        return remote(
            wbuf.at[unit], wbuf.at[unit], w_send.at[way, unit], w_recv.at[unit],
            me + (2 if way else -2), sec,
        )

    for c in range(parts):
        own_loads[c].wait()

        @pl.when(spot < line - 1)
        def _():
            w_copy(1, spot, c).start()

        @pl.when(spot > 0)
        def _():
            w_copy(0, spot, c).start()

    hid_copy = remote(hidden, hid_in, x_send.at[0], x_recv.at[0], me, before)
    gout_copy = remote(grad_out, gout_in, x_send.at[1], x_recv.at[1], me, before)
    hid_copy.start()
    gout_copy.start()

    def take(dist, c):
        @pl.when(spot - dist >= 0)
        def _():
            w_copy(1, spot - dist, c).wait_recv()

            @pl.when(spot < line - 1)
            def _():
                w_copy(1, spot - dist, c).start()

        @pl.when(spot + dist < line)
        def _():
            w_copy(0, spot + dist, c).wait_recv()

            @pl.when(spot > 0)
            def _():
                w_copy(0, spot + dist, c).start()

    for c in range(parts):
        if line > 2:
            take(1, c)

    @pl.loop(1, shards)
    def _(off):
        source = lax.rem(me + off, shards)
        kv_copy(source, source).wait_recv()

    q_load.wait()
    gh_load.wait()
    factor = HEAD_DIM ** (-0.5)

    def qg_copy(c):
        rows = pl.ds(c * STRETCH, STRETCH)
        return remote(
            qg.at[0, rows], qg.at[1, rows], qg_send.at[c], qg_recv.at[c], partner, sec
        )

    @pl.loop(0, stretches)
    def _(c):
        rows = pl.ds(pl.multiple_of(c * STRETCH, STRETCH), STRETCH)
        first, second = place[c, 0], place[c, 1]
        for h in range(heads):
            cols = slice(h * HEAD_DIM, (h + 1) * HEAD_DIM)
            vcols = slice(qwidth + h * HEAD_DIM, qwidth + (h + 1) * HEAD_DIM)
            keys = jnp.concatenate([fetched[first, :, cols], fetched[second, :, cols]], axis=0)
            values = jnp.concatenate([fetched[first, :, vcols], fetched[second, :, vcols]], axis=0)
            scores = lax.dot_general(
                q_v[rows, cols], keys, NT, preferred_element_type=jnp.float32
            ) * factor
            dprob = lax.dot_general(
                gh_v[rows, cols], values, NT, preferred_element_type=jnp.float32
            )
            exps = jnp.exp(scores - jnp.max(scores, axis=-1, keepdims=True))
            probs = exps / jnp.sum(exps, axis=-1, keepdims=True)
            inner = jnp.sum(probs * dprob, axis=-1, keepdims=True)
            dscore = (factor * probs * (dprob - inner)).astype(jnp.bfloat16)
            qg[0, rows, cols] = lax.dot_general(
                dscore, keys, NN, preferred_element_type=jnp.float32
            ).astype(jnp.bfloat16)
        qg_copy(c).start()

    @pl.loop(0, stretches)
    def _(c):
        qg_copy(c).wait_recv()

    def g_copy(which, block, c):
        unit = (block * 2 + side) * parts + c
        return remote(
            stage.at[which, block * parts + c], g_in.at[unit],
            g_send.at[which, block * parts + c], g_recv.at[unit],
            partner if which else me, before,
        )

    def work(block, c):
        unit = block * parts + c
        scale = gain[(block * 2 + side) * parts + c]
        for which in (1, 0):
            product = lax.dot_general(
                qg[which], wbuf[unit], NT, preferred_element_type=jnp.float32
            )
            stage[which, unit] = (product * scale).astype(jnp.bfloat16)
            g_copy(which, block, c).start()

    @pl.loop(0, parts)
    def _(c):
        work(spot, c)

    @pl.loop(1, line)
    def _(dist):
        @pl.when(dist + 1 < line - 1)
        def _():
            for c in range(parts):
                take(dist + 1, c)

        @pl.loop(0, parts)
        def _(c):
            @pl.when(dist == line - 1)
            def _():
                take(dist, c)

            @pl.loop(0, 2)
            def _(way):
                block = spot + dist * (2 * way - 1)

                @pl.when((block >= 0) & (block < line))
                def _():
                    work(block, c)

    hid_copy.wait_recv()
    gout_copy.wait_recv()
    units = shards * parts

    @pl.loop(0, units)
    def _(unit):
        remote(
            stage.at[0, 0], g_in.at[unit], g_send.at[0, 0], g_recv.at[unit], me, before
        ).wait_recv()

    tile = 32
    tiles = tokens // tile

    def out_copy(i):
        rows = pl.ds(i * tile, tile)
        return pltpu.make_async_copy(gout_in.at[rows], out.at[rows], out_sem.at[i])

    @pl.loop(0, tiles)
    def _(i):
        rows = pl.ds(pl.multiple_of(i * tile, tile), tile)
        squares = jnp.zeros((tile, piece), jnp.float32)
        inners = jnp.zeros((tile, piece), jnp.float32)
        for unit in range(units):
            x = hid_in[rows, unit * piece:(unit + 1) * piece].astype(jnp.float32)
            g = g_in[unit, rows, :].astype(jnp.float32)
            squares += x * x
            inners += g * x
        inv = lax.rsqrt(jnp.sum(squares, axis=-1, keepdims=True) / width + norm_eps)
        mean = jnp.sum(inners, axis=-1, keepdims=True) * inv / width
        slope = inv * inv * mean
        for unit in range(units):
            cols = slice(unit * piece, (unit + 1) * piece)
            x = hid_in[rows, cols].astype(jnp.float32)
            g = g_in[unit, rows, :].astype(jnp.float32)
            total = gout_in[rows, cols].astype(jnp.float32) + (inv * g - slope * x)
            gout_in[rows, cols] = total.astype(jnp.bfloat16)
        out_copy(i).start()

    @pl.loop(1, shards)
    def _(off):
        to = lax.rem(me + off, shards)
        req_copy(to, me).wait_send()
        kv_copy(to, me).wait_send()

    hid_copy.wait_send()
    gout_copy.wait_send()

    @pl.loop(0, stretches)
    def _(c):
        qg_copy(c).wait_send()

    @pl.loop(0, line)
    def _(block):
        for c in range(parts):
            g_copy(0, block, c).wait_send()
            g_copy(1, block, c).wait_send()

            @pl.when((block <= spot) & (spot < line - 1))
            def _():
                w_copy(1, block, c).wait_send()

            @pl.when((block >= spot) & (spot > 0))
            def _():
                w_copy(0, block, c).wait_send()

    @pl.loop(0, tiles)
    def _(i):
        out_copy(i).wait()


def local(
    sections, hidden, norm_gain, queries, cache, nbr_shard, nbr_slot, grad_heads, grad_out,
    query_weight,
):
    shards = lax.axis_size("stretch")
    _, tokens, qwidth = queries.shape
    width = hidden.shape[2]
    stretches, neighbours = nbr_shard.shape
    capacity = (neighbours * stretches + shards - 1) // shards
    _, slots, span, _ = cache.shape
    owners = nbr_shard.reshape(-1)
    slot_rank = slot_ranks(owners)
    wanted = request_table(owners, slot_rank, nbr_slot.reshape(-1), shards, capacity)
    wanted = jnp.pad(wanted[:, None, :], ((0, 0), (0, 7), (0, 128 - capacity)))
    place = (owners * capacity + slot_rank).reshape(stretches, neighbours)
    rows = query_weight.shape[1]
    parts = 2 if rows % 512 == 0 else 1
    piece = rows // parts
    line = shards // 2
    units = shards * parts
    bf16 = jnp.bfloat16
    dma = pltpu.SemaphoreType.DMA
    vmem = pl.BlockSpec(memory_space=pltpu.VMEM)
    hbm = pl.BlockSpec(memory_space=pl.ANY)
    out = pl.pallas_call(
        functools.partial(kernel, shards, sections, capacity, parts),
        out_shape=jax.ShapeDtypeStruct((tokens, width), bf16),
        in_specs=[vmem, pl.BlockSpec(memory_space=pltpu.SMEM), vmem] + [hbm] * 6,
        out_specs=hbm,
        scratch_shapes=[
            pltpu.VMEM((shards, 8, 128), jnp.int32),
            pltpu.SMEM((shards, 8, 128), jnp.int32),
            pltpu.VMEM((slots, span, 2 * qwidth), bf16),
            pltpu.VMEM((shards * capacity, span, 2 * qwidth), bf16),
            pltpu.VMEM((shards * capacity, span, 2 * qwidth), bf16),
            pltpu.VMEM((tokens, qwidth), bf16),
            pltpu.VMEM((tokens, qwidth), bf16),
            pltpu.VMEM((line * parts, piece, qwidth), bf16),
            pltpu.VMEM((2, tokens, qwidth), bf16),
            pltpu.VMEM((2, line * parts, tokens, piece), bf16),
            pltpu.VMEM((units, tokens, piece), bf16),
            pltpu.VMEM((tokens, width), bf16),
            pltpu.VMEM((tokens, width), bf16),
            dma((4 + parts,)),
            dma((shards,)),
            dma((shards,)),
            dma((shards,)),
            dma((shards,)),
            dma((2, line * parts)),
            dma((line * parts,)),
            dma((stretches,)),
            dma((stretches,)),
            dma((2, line * parts)),
            dma((units,)),
            dma((2,)),
            dma((2,)),
            dma((tokens // 32,)),
        ],
        compiler_params=pltpu.CompilerParams(
            collective_id=0, has_side_effects=True, vmem_limit_bytes=60 * 1024 * 1024
        ),
        cost_estimate=pl.CostEstimate(
            flops=2 * tokens * qwidth * width, bytes_accessed=24 << 20, transcendentals=0
        ),
    )(
        wanted, place, norm_gain[0].reshape(units, 1, piece), hidden[0], queries[0], cache[0],
        grad_heads[0], grad_out[0], query_weight[0],
    )
    return out[None]


def solution(mesh):
    in_specs = (
        P("section", "stretch", None),
        P("section", None),
        P("section", "stretch", None),
        P("section", "stretch", None, None),
        P("stretch", None),
        P("stretch", None),
        P("section", "stretch", None),
        P("section", "stretch", None),
        P("section", "stretch", None),
    )
    return jax.shard_map(
        functools.partial(local, mesh.shape["section"]), mesh=mesh, in_specs=in_specs,
        out_specs=P("section", "stretch", None), check_vma=False,
    )
```

time: 399 us -> 270 us (0.68)
  waiting for transfers between devices: 301 us -> 0 us
  Pallas kernels: 0 us -> 262 us
  matrix products: 27.3 us -> 0 us
  local copies, waits for them, and re-layouts: 23.3 us -> 7.16 us
  other arithmetic: 16.7 us -> 0.95 us
  between operations: 13.5 us -> 0.02 us
  blocking collectives: 11.5 us -> 0 us
  starting transfers between devices: 5.19 us -> 0 us
    pallas_call x0 -> x1, Pallas kernels: none -> 262 us  [local(): pl.pallas_call(functools.partial(kernel, shards, sections, capacity, part...]
    all_to_all x1 -> x0, waiting for transfers between devices: 171 us -> none  [local(): lax.all_to_all(picked, 'stretch', split_axis=0, concat_axis=0, tiled=True)]
    all_gather x1 -> x0, waiting for transfers between devices: 82.3 us -> none  [local(): lax.all_gather(weight_rows, 'stretch', axis=0, tiled=True)]
    ppermute x1 -> x0, waiting for transfers between devices: 47.5 us -> none  [passed_along(): return lax.ppermute(value, axis, pairs)]
    dot_general x4 -> x0, matrix products: 27.3 us -> none  [the longest x1 16.3 us: local(): lax.dot_general(query_grad, lax.all_gather(weight_rows, 'stretch', axis=0...]
    all_to_all x1 -> x0, blocking collectives: 11.5 us -> none  [local(): lax.all_to_all(wanted, 'stretch', split_axis=0, concat_axis=0, tiled=True)]
    gather x2 -> x0, local copies, waits for them, and re-layouts: 10.5 us -> none  [the longest x1 5.44 us: local(): cache_table[jnp.maximum(lax.all_to_all(wanted, 'stretch', split_axis=0, c...]
    div x2 -> x0, other arithmetic: 8.45 us -> none  [the longest x1 8.44 us: local(): attn_probs = exp_scores / jnp.sum(exp_scores, axis=-1, keepdims=True)]
  transfers between devices with their start and end apart: 3 -> 0, of which waited for: 3 -> 0; matrix products, arithmetic and copies ran while one was open for 11% -> 0% of each run, Pallas kernels for 0% -> 0%
where the time goes in v1:
time: 270 us
  Pallas kernels  262 us (97%)
  local copies, waits for them, and re-layouts  7.16 us (3%)
    pallas_call x1, Pallas kernels, local(): pl.pallas_call(functools.partial(kernel, shards, sections, capacity, part...  262 us
    unnamed x3, local copies, waits for them, and re-layouts  6.2 us

profile of v1, /device:TPU:1, one launch (start us, length us, event | category | flops | bytes accessed | tf_op | source)
XLA Modules:
  0.0 269.8 jit_solution(11961842015807214572)
XLA Ops:
  0.0 0.8 copy.18
  0.8 0.1 eq.51
  0.8 0.2 convert_reduce_fusion
  1.0 0.1 reduce_sum.22
  1.1 0.6 multiply_add_fusion.place
  1.7 0.8 copy.19
  2.5 0.1 broadcast_in_dim.25
  2.6 0.1 select_reduce_fusion
  2.7 0.1 copy.20
  2.8 0.6 pad.4.wanted
  3.4 261.7 %shard_map.91 = bf16[512,4096]{1,0:T(8,128)(2,1)} custom-call(s32[8,8,128]{2,1,0:T(8,128)} %pad.4.wanted, s32[8,2]{1,0:T(8,128)} %multiply_add_fusion.place, f32[16,1,256]{2,1,0:T(1,128)} %bitcast.17, bf16[512,4096]{1,0:T(8,128)(2,1)} %bitcast.11, bf16[512,2048]{1,0:T(8,128)(2,1)} %bitcast.14, bf16[16,32,4096]{2,1,0:T(8,128)(2,1)} %bitcast.12, ...), custom_call_target="tpu_custom_call" | custom-call | flops 8589934592 | bytes 25165824 | tf_op jit(solution)/shard_map/pallas_call | solution.py:350
  265.1 4.7 %copy.23 = bf16[1,512,4096]{2,1,0:T(8,128)(2,1)} copy(bf16[1,512,4096]{2,1,0:T(8,128)(2,1)} %bitcast.9) | data formatting | bytes 8388608
  (2 shorter events, 0.0 us)

commit v2 on v1

--- a/solution.py
+++ b/solution.py
@@ -32,7 +32,7 @@
 
 
 def kernel(
-    shards, sections, capacity, parts,
+    shards, sections, capacity, parts, subs,
     wanted, place, gain, hidden, queries, cache, grads, grad_out, weight,
     out,
     req, req_s, cache_v, picked, fetched, q_v, gh_v, wbuf, qg, stage, g_in, hid_in, gout_in,
@@ -53,6 +53,8 @@
     stretches = tokens // STRETCH
     span = cache.shape[1]
     piece = weight.shape[0] // parts
+    chunks = parts * subs
+    chunk = piece // subs
 
     def remote(src, dst, ssem, rsem, stretch, section):
         return pltpu.make_async_remote_copy(
@@ -89,9 +91,9 @@
     gh_load.start()
     own_loads = [
         pltpu.make_async_copy(
-            weight.at[pl.ds(c * piece, piece)], wbuf.at[spot * parts + c], load_sem.at[4 + c]
-        )
-        for c in range(parts)
+            weight.at[pl.ds(q * chunk, chunk)], wbuf.at[spot * chunks + q], load_sem.at[4 + q]
+        )
+        for q in range(chunks)
     ]
     for load in own_loads:
         load.start()
@@ -123,54 +125,66 @@
     for k in range(capacity):
         fetched[me * capacity + k] = cache_v[req_s[me, 0, k]]
 
-    def w_copy(way, block, c):
-        unit = block * parts + c
+    def w_copy(way, block, q):
+        unit = block * chunks + q
         return remote(
             wbuf.at[unit], wbuf.at[unit], w_send.at[way, unit], w_recv.at[unit],
             me + (2 if way else -2), sec,
         )
 
-    for c in range(parts):
-        own_loads[c].wait()
-
-        @pl.when(spot < line - 1)
-        def _():
-            w_copy(1, spot, c).start()
-
-        @pl.when(spot > 0)
-        def _():
-            w_copy(0, spot, c).start()
+    onward = (spot > 0, spot < line - 1)
+    at_end = (
+        (spot == line - 1) | (spot == 1), (spot == 0) | (spot == line - 2)
+    )
+
+    def first_hop(q, early):
+        for way in (0, 1):
+            if q == 0:
+                go = onward[way]
+            elif early:
+                go = onward[way] & at_end[way]
+            else:
+                go = onward[way] & jnp.logical_not(at_end[way])
+
+            @pl.when(go)
+            def _():
+                w_copy(way, spot, q).start()
+
+    for q in range(chunks):
+        own_loads[q].wait()
+        first_hop(q, True)
 
     hid_copy = remote(hidden, hid_in, x_send.at[0], x_recv.at[0], me, before)
     gout_copy = remote(grad_out, gout_in, x_send.at[1], x_recv.at[1], me, before)
     hid_copy.start()
     gout_copy.start()
 
-    def take(dist, c):
-        @pl.when(spot - dist >= 0)
-        def _():
-            w_copy(1, spot - dist, c).wait_recv()
-
-            @pl.when(spot < line - 1)
-            def _():
-                w_copy(1, spot - dist, c).start()
-
-        @pl.when(spot + dist < line)
-        def _():
-            w_copy(0, spot + dist, c).wait_recv()
-
-            @pl.when(spot > 0)
-            def _():
-                w_copy(0, spot + dist, c).start()
-
-    for c in range(parts):
-        if line > 2:
-            take(1, c)
-
-    @pl.loop(1, shards)
-    def _(off):
-        source = lax.rem(me + off, shards)
-        kv_copy(source, source).wait_recv()
+    def passing(dist, q):
+        for way, block in ((1, spot - dist), (0, spot + dist)):
+            @pl.when(onward[way] & (block >= 0) & (block < line))
+            def _():
+                w_copy(way, block, q).wait_recv()
+                w_copy(way, block, q).start()
+
+    def ending(dist, q):
+        for way, block in ((1, spot - dist), (0, spot + dist)):
+            @pl.when(jnp.logical_not(onward[way]) & (block >= 0) & (block < line))
+            def _():
+                w_copy(way, block, q).wait_recv()
+
+    def rows_from(first, last):
+        @pl.loop(first, last)
+        def _(off):
+            source = lax.rem(me + off, shards)
+            kv_copy(source, source).wait_recv()
+
+    passing(1, 0)
+    rows_from(1, shards // 2)
+    if chunks > 1:
+        first_hop(1, False)
+    rows_from(shards // 2, shards)
+    for q in range(2, chunks):
+        first_hop(q, False)
 
     q_load.wait()
     gh_load.wait()
@@ -205,6 +219,13 @@
                 dscore, keys, NN, preferred_element_type=jnp.float32
             ).astype(jnp.bfloat16)
         qg_copy(c).start()
+        for q in range(1, chunks):
+            @pl.when(c == min(q * stretches // chunks + 1, stretches - 1))
+            def _():
+                passing(1, q)
+
+    for q in range(subs):
+        passing(2, q)
 
     @pl.loop(0, stretches)
     def _(c):
@@ -220,36 +241,33 @@
 
     def work(block, c):
         unit = block * parts + c
+        rows = wbuf[pl.ds(unit * subs, subs)].reshape(piece, qwidth)
         scale = gain[(block * 2 + side) * parts + c]
         for which in (1, 0):
             product = lax.dot_general(
-                qg[which], wbuf[unit], NT, preferred_element_type=jnp.float32
+                qg[which], rows, NT, preferred_element_type=jnp.float32
             )
             stage[which, unit] = (product * scale).astype(jnp.bfloat16)
             g_copy(which, block, c).start()
 
-    @pl.loop(0, parts)
-    def _(c):
-        work(spot, c)
-
-    @pl.loop(1, line)
+    @pl.loop(0, line)
     def _(dist):
-        @pl.when(dist + 1 < line - 1)
-        def _():
-            for c in range(parts):
-                take(dist + 1, c)
-
         @pl.loop(0, parts)
         def _(c):
-            @pl.when(dist == line - 1)
-            def _():
-                take(dist, c)
+            for sub in range(subs):
+                @pl.when((dist > 0) | (c > 0))
+                def _():
+                    passing(dist + 2, c * subs + sub)
+
+                @pl.when(dist > 0)
+                def _():
+                    ending(dist, c * subs + sub)
 
             @pl.loop(0, 2)
             def _(way):
                 block = spot + dist * (2 * way - 1)
 
-                @pl.when((block >= 0) & (block < line))
+                @pl.when((block >= 0) & (block < line) & ((dist > 0) | (way > 0)))
                 def _():
                     work(block, c)
 
@@ -310,13 +328,14 @@
             g_copy(0, block, c).wait_send()
             g_copy(1, block, c).wait_send()
 
+        for q in range(chunks):
             @pl.when((block <= spot) & (spot < line - 1))
             def _():
-                w_copy(1, block, c).wait_send()
+                w_copy(1, block, q).wait_send()
 
             @pl.when((block >= spot) & (spot > 0))
             def _():
-                w_copy(0, block, c).wait_send()
+                w_copy(0, block, q).wait_send()
 
     @pl.loop(0, tiles)
     def _(i):
@@ -340,15 +359,17 @@
     place = (owners * capacity + slot_rank).reshape(stretches, neighbours)
     rows = query_weight.shape[1]
     parts = 2 if rows % 512 == 0 else 1
+    subs = 2 if rows % 512 == 0 else 1
     piece = rows // parts
     line = shards // 2
+    chunks = parts * subs
     units = shards * parts
     bf16 = jnp.bfloat16
     dma = pltpu.SemaphoreType.DMA
     vmem = pl.BlockSpec(memory_space=pltpu.VMEM)
     hbm = pl.BlockSpec(memory_space=pl.ANY)
     out = pl.pallas_call(
-        functools.partial(kernel, shards, sections, capacity, parts),
+        functools.partial(kernel, shards, sections, capacity, parts, subs),
         out_shape=jax.ShapeDtypeStruct((tokens, width), bf16),
         in_specs=[vmem, pl.BlockSpec(memory_space=pltpu.SMEM), vmem] + [hbm] * 6,
         out_specs=hbm,
@@ -360,19 +381,19 @@
             pltpu.VMEM((shards * capacity, span, 2 * qwidth), bf16),
             pltpu.VMEM((tokens, qwidth), bf16),
             pltpu.VMEM((tokens, qwidth), bf16),
-            pltpu.VMEM((line * parts, piece, qwidth), bf16),
+            pltpu.VMEM((line * chunks, piece // subs, qwidth), bf16),
             pltpu.VMEM((2, tokens, qwidth), bf16),
             pltpu.VMEM((2, line * parts, tokens, piece), bf16),
             pltpu.VMEM((units, tokens, piece), bf16),
             pltpu.VMEM((tokens, width), bf16),
             pltpu.VMEM((tokens, width), bf16),
-            dma((4 + parts,)),
+            dma((4 + chunks,)),
             dma((shards,)),
             dma((shards,)),
             dma((shards,)),
             dma((shards,)),
-            dma((2, line * parts)),
-            dma((line * parts,)),
+            dma((2, line * chunks)),
+            dma((line * chunks,)),
             dma((stretches,)),
             dma((stretches,)),
             dma((2, line * parts)),

time: 270 us -> 248 us (0.919)
  the two profiles are of different devices: /device:TPU:1 before, /device:TPU:15 now
where the time goes in v2:
time: 248 us
  Pallas kernels  240 us (97%)
  local copies, waits for them, and re-layouts  7.16 us (3%)
    pallas_call x1, Pallas kernels, local(): pl.pallas_call(functools.partial(kernel, shards, sections, capacity, part...  240 us
    unnamed x3, local copies, waits for them, and re-layouts  6.2 us

profile of v2, /device:TPU:15, one launch (start us, length us, event | category | flops | bytes accessed | tf_op | source)
XLA Modules:
  0.0 248.2 jit_solution(3345921942231000764)
XLA Ops:
  0.0 0.8 copy.18
  0.8 0.1 eq.51
  0.8 0.2 convert_reduce_fusion
  1.0 0.1 reduce_sum.22
  1.1 0.6 multiply_add_fusion.place
  1.7 0.8 copy.19
  2.5 0.1 broadcast_in_dim.25
  2.6 0.1 select_reduce_fusion
  2.7 0.1 copy.20
  2.8 0.6 pad.4.wanted
  3.4 240.1 %shard_map.91 = bf16[512,4096]{1,0:T(8,128)(2,1)} custom-call(s32[8,8,128]{2,1,0:T(8,128)} %pad.4.wanted, s32[8,2]{1,0:T(8,128)} %multiply_add_fusion.place, f32[16,1,256]{2,1,0:T(1,128)} %bitcast.17, bf16[512,4096]{1,0:T(8,128)(2,1)} %bitcast.11, bf16[512,2048]{1,0:T(8,128)(2,1)} %bitcast.14, bf16[16,32,4096]{2,1,0:T(8,128)(2,1)} %bitcast.12, ...), custom_call_target="tpu_custom_call" | custom-call | flops 8589934592 | bytes 25165824 | tf_op jit(solution)/shard_map/pallas_call | solution.py:371
  243.5 4.7 %copy.23 = bf16[1,512,4096]{2,1,0:T(8,128)(2,1)} copy(bf16[1,512,4096]{2,1,0:T(8,128)(2,1)} %bitcast.9) | data formatting | bytes 8388608
  (2 shorter events, 0.0 us)

commit v3 on v2

--- a/solution.py
+++ b/solution.py
@@ -35,7 +35,7 @@
     shards, sections, capacity, parts, subs,
     wanted, place, gain, hidden, queries, cache, grads, grad_out, weight,
     out,
-    req, req_s, cache_v, picked, fetched, q_v, gh_v, wbuf, qg, stage, g_in, hid_in, gout_in,
+    req, req_s, cache_v, picked, fetched, q_v, gh_v, wbuf, qg, stage, g_in, hid_in, gout_in, sums,
     load_sem, req_send, req_recv, kv_send, kv_recv, w_send, w_recv, qg_send, qg_recv,
     g_send, g_recv, x_send, x_recv, out_sem,
 ):
@@ -224,12 +224,6 @@
             def _():
                 passing(1, q)
 
-    for q in range(subs):
-        passing(2, q)
-
-    @pl.loop(0, stretches)
-    def _(c):
-        qg_copy(c).wait_recv()
 
     def g_copy(which, block, c):
         unit = (block * 2 + side) * parts + c
@@ -250,37 +244,74 @@
             stage[which, unit] = (product * scale).astype(jnp.bfloat16)
             g_copy(which, block, c).start()
 
-    @pl.loop(0, line)
-    def _(dist):
-        @pl.loop(0, parts)
-        def _(c):
+    def shift(q):
+        return (-parts, 0, 1, 3)[q] if chunks == 4 else q // subs
+
+    @pl.loop(0, line * parts)
+    def _(step):
+        dist, c = step // parts, lax.rem(step, parts)
+        for q in range(chunks):
+            due = step - shift(q)
+
+            @pl.when((due >= parts) & (lax.rem(due, parts) == 0))
+            def _():
+                passing(due // parts + 1, q)
+
+        @pl.when(step == 0)
+        def _():
+            @pl.loop(0, stretches)
+            def _(c):
+                qg_copy(c).wait_recv()
+
+        @pl.when(dist > 0)
+        def _():
             for sub in range(subs):
-                @pl.when((dist > 0) | (c > 0))
-                def _():
-                    passing(dist + 2, c * subs + sub)
-
-                @pl.when(dist > 0)
-                def _():
-                    ending(dist, c * subs + sub)
-
-            @pl.loop(0, 2)
-            def _(way):
-                block = spot + dist * (2 * way - 1)
-
-                @pl.when((block >= 0) & (block < line) & ((dist > 0) | (way > 0)))
-                def _():
-                    work(block, c)
+                ending(dist, c * subs + sub)
+
+        @pl.loop(0, 2)
+        def _(way):
+            block = spot + dist * (2 * way - 1)
+
+            @pl.when((block >= 0) & (block < line) & ((dist > 0) | (way > 0)))
+            def _():
+                work(block, c)
 
     hid_copy.wait_recv()
-    gout_copy.wait_recv()
     units = shards * parts
-
-    @pl.loop(0, units)
-    def _(unit):
+    sums[...] = jnp.zeros_like(sums)
+
+    def add_unit(unit):
         remote(
             stage.at[0, 0], g_in.at[unit], g_send.at[0, 0], g_recv.at[unit], me, before
         ).wait_recv()
 
+        @pl.loop(0, tokens // STRETCH)
+        def _(i):
+            rows = pl.ds(pl.multiple_of(i * STRETCH, STRETCH), STRETCH)
+            squares, inners = sums[0, rows], sums[1, rows]
+            for k in range(piece // 128):
+                cols = pl.ds(pl.multiple_of(unit * piece + k * 128, 128), 128)
+                x = hid_in[rows, cols].astype(jnp.float32)
+                g = g_in[unit, rows, k * 128:(k + 1) * 128].astype(jnp.float32)
+                squares += x * x
+                inners += g * x
+            sums[0, rows] = squares
+            sums[1, rows] = inners
+
+    @pl.loop(0, line * parts)
+    def _(step):
+        dist, c = step // parts, lax.rem(step, parts)
+
+        @pl.loop(0, 4)
+        def _(k):
+            way, half = k // 2, lax.rem(k, 2)
+            block = spot + dist * (2 * way - 1)
+
+            @pl.when((block >= 0) & (block < line) & ((dist > 0) | (way > 0)))
+            def _():
+                add_unit((block * 2 + half) * parts + c)
+
+    gout_copy.wait_recv()
     tile = 32
     tiles = tokens // tile
 
@@ -291,15 +322,8 @@
     @pl.loop(0, tiles)
     def _(i):
         rows = pl.ds(pl.multiple_of(i * tile, tile), tile)
-        squares = jnp.zeros((tile, piece), jnp.float32)
-        inners = jnp.zeros((tile, piece), jnp.float32)
-        for unit in range(units):
-            x = hid_in[rows, unit * piece:(unit + 1) * piece].astype(jnp.float32)
-            g = g_in[unit, rows, :].astype(jnp.float32)
-            squares += x * x
-            inners += g * x
-        inv = lax.rsqrt(jnp.sum(squares, axis=-1, keepdims=True) / width + norm_eps)
-        mean = jnp.sum(inners, axis=-1, keepdims=True) * inv / width
+        inv = lax.rsqrt(jnp.sum(sums[0, rows], axis=-1, keepdims=True) / width + norm_eps)
+        mean = jnp.sum(sums[1, rows], axis=-1, keepdims=True) * inv / width
         slope = inv * inv * mean
         for unit in range(units):
             cols = slice(unit * piece, (unit + 1) * piece)
@@ -387,6 +411,7 @@
             pltpu.VMEM((units, tokens, piece), bf16),
             pltpu.VMEM((tokens, width), bf16),
             pltpu.VMEM((tokens, width), bf16),
+            pltpu.VMEM((2, tokens, 128), jnp.float32),
             dma((4 + chunks,)),
             dma((shards,)),
             dma((shards,)),

time: 248 us -> 238 us (0.960)
  the two profiles are of different devices: /device:TPU:15 before, /device:TPU:1 now
where the time goes in v3:
time: 238 us
  Pallas kernels  230 us (97%)
  local copies, waits for them, and re-layouts  7.16 us (3%)
    pallas_call x1, Pallas kernels, local(): pl.pallas_call(functools.partial(kernel, shards, sections, capacity, part...  230 us
    unnamed x3, local copies, waits for them, and re-layouts  6.2 us

profile of v3, /device:TPU:1, one launch (start us, length us, event | category | flops | bytes accessed | tf_op | source)
XLA Modules:
  0.0 237.8 jit_solution(13461378354942901168)
XLA Ops:
  0.0 0.8 copy.18
  0.8 0.1 eq.51
  0.8 0.2 convert_reduce_fusion
  1.0 0.1 reduce_sum.22
  1.1 0.6 multiply_add_fusion.place
  1.7 0.8 copy.19
  2.5 0.1 broadcast_in_dim.25
  2.6 0.1 select_reduce_fusion
  2.7 0.1 copy.20
  2.8 0.6 pad.4.wanted
  3.4 229.7 %shard_map.91 = bf16[512,4096]{1,0:T(8,128)(2,1)} custom-call(s32[8,8,128]{2,1,0:T(8,128)} %pad.4.wanted, s32[8,2]{1,0:T(8,128)} %multiply_add_fusion.place, f32[16,1,256]{2,1,0:T(1,128)} %bitcast.17, bf16[512,4096]{1,0:T(8,128)(2,1)} %bitcast.11, bf16[512,2048]{1,0:T(8,128)(2,1)} %bitcast.14, bf16[16,32,4096]{2,1,0:T(8,128)(2,1)} %bitcast.12, ...), custom_call_target="tpu_custom_call" | custom-call | flops 8589934592 | bytes 25165824 | tf_op jit(solution)/shard_map/pallas_call | solution.py:395
  233.1 4.7 %copy.23 = bf16[1,512,4096]{2,1,0:T(8,128)(2,1)} copy(bf16[1,512,4096]{2,1,0:T(8,128)(2,1)} %bitcast.9) | data formatting | bytes 8388608
  (2 shorter events, 0.0 us)
